TPU v7x, 32 devices: a whole 2x2x4 slice. The times are simulated.
32 devices in a mesh: parts: 2 (over y), blk: 4 (over x, core), rep: 4 (over z).
Axes of the slice: x: 2, y: 2, z: 4, core: 2. Of those that a mesh axis runs over, the one named last changes fastest.
Arguments:
- features: float32 [8192, 128], P(('parts', 'blk', 'rep')), parts along dimension 0, may hold values from -6 to 6
- neighbour_mean: float32 [8192, 128], P(('parts', 'blk', 'rep')), parts along dimension 0, may hold values from -6 to 6
- out_grad: float32 [8192, 256], P(('parts', 'blk', 'rep')), parts along dimension 0, may hold values from -6 to 6
- self_weight: float32 [128, 256], replicated, may hold values from -0.5 to 0.5
- neigh_weight: float32 [128, 256], replicated, may hold values from -0.5 to 0.5
- bias: float32 [256], replicated, may hold values from -4 to 4
- tile_values: float32 [8, 4, 4, 10, 128, 128], P(('parts', 'blk'), 'rep'), parts along dimension 0, may hold values from 0 to 0.03
- tile_coords: int32 [8, 4, 4, 10, 2], P(('parts', 'blk'), 'rep'), parts along dimension 0, may hold values from 0 to 7, as said below
- tile_counts: int32 [8, 4, 4], P(('parts', 'blk'), 'rep'), parts along dimension 0, may hold values from 1 to 10
Outputs:
- feature_grad: float32 [8192, 128], P(('parts', 'blk', 'rep')), parts along dimension 0
- self_grad: float32 [256, 256], P('parts'), parts along dimension 0
- neigh_grad: float32 [256, 256], P('parts'), parts along dimension 0
- bias_grad: float32 [512], P('parts'), parts along dimension 0
There are 2 independent parts, one for each index of `parts`. A program takes and returns all parts, laid end to end along the dimension named above; an argument that names none is the same for every part. Nothing has to cross between parts.
Inputs may be any that keep to these rules, and one draw needn't show every extreme that they name: tile_coords[..., 0] is below 8 and tile_coords[..., 1] below 2; within one list of 10 slots the pairs are distinct.
All inputs are finite; a program needn't handle non-finite values.
Results may differ from a plain program's by a relative error of at most 0.0003.
Values sent between devices are 32-bit elements; how exact they have to be, the bound alone decides.
A program may use at most 64 MiB of HBM per device.

v0:
```python
import jax
import jax.numpy as jnp
from jax import lax
from jax.sharding import PartitionSpec as P

F = 128
TILE = 128
TR = 2
TCAP = 10


def from_behind(block, axis, distance):
    devices = range(lax.axis_size(axis))
    route = [((i - distance) % len(devices), i) for i in devices]
    return lax.ppermute(block, axis, route)


def block_terms(tile_rows, tile_block, coords, tile_count):
    top_precision = lax.Precision.HIGHEST
    chosen_tiles = jnp.take(tile_rows, coords[:, 0], axis=0)
    tile_products = jnp.einsum("tab,taf->tbf", tile_block, chosen_tiles, precision=top_precision)
    live = jnp.arange(TCAP, dtype=jnp.int32) < tile_count
    select_tile = (
        (coords[:, 1][:, None] == jnp.arange(TR, dtype=jnp.int32)[None, :]) & live[:, None]
    ).astype(jnp.float32)
    summed_terms = jnp.einsum("ip,iwe->pwe", select_tile, tile_products, precision=top_precision)
    return summed_terms.reshape(TR * TILE, F)


def on_device(
    features,
    neighbour_mean,
    out_grad,
    self_weight,
    neigh_weight,
    bias,
    tile_values,
    tile_coords,
    tile_counts,
):
    top_precision = lax.Precision.HIGHEST
    pre = jnp.dot(
        features, self_weight, precision=top_precision, preferred_element_type=jnp.float32
    )
    pre = (
        pre
        + jnp.dot(
            neighbour_mean,
            neigh_weight,
            precision=top_precision,
            preferred_element_type=jnp.float32,
        )
        + bias
    )
    sigmoid_pre = jax.nn.sigmoid(pre)
    d_pre = out_grad * sigmoid_pre * (1.0 + pre * (1.0 - sigmoid_pre))
    d_agg = jnp.dot(
        d_pre, neigh_weight.T, precision=top_precision, preferred_element_type=jnp.float32
    )
    block_grad = lax.all_gather(d_agg, "rep", axis=0, tiled=True)
    tile_rows = block_grad.reshape(block_grad.shape[0] // TILE, TILE, F)
    tiles_here = tile_values[0, 0]
    coords_here = tile_coords[0, 0]
    counts_here = tile_counts[0, 0]
    cycle_size = lax.axis_size("blk")
    home_block = lax.axis_index("blk")

    def terms_at(step_index):
        column_block = (home_block - 1 - step_index) % cycle_size
        tile_block = lax.dynamic_index_in_dim(tiles_here, column_block, 0, keepdims=False)
        coords = lax.dynamic_index_in_dim(coords_here, column_block, 0, keepdims=False)
        tile_count = lax.dynamic_index_in_dim(counts_here, column_block, 0, keepdims=False)
        return block_terms(tile_rows, tile_block, coords, tile_count)

    def cycle_step(step_index, partial_sum):
        return from_behind(partial_sum, "blk", 1) + terms_at(step_index)

    neighbour_grad = lax.fori_loop(1, cycle_size, cycle_step, terms_at(jnp.int32(0)))
    feature_grad = (
        jnp.dot(d_pre, self_weight.T, precision=top_precision, preferred_element_type=jnp.float32)
        + neighbour_grad
    )
    self_local = jnp.dot(
        features.T, d_pre, precision=top_precision, preferred_element_type=jnp.float32
    )
    neighbour_part = jnp.dot(
        neighbour_mean.T, d_pre, precision=top_precision, preferred_element_type=jnp.float32
    )
    bias_local = jnp.sum(d_pre, axis=0)
    self_grad, neigh_grad, bias_grad = lax.psum(
        (self_local, neighbour_part, bias_local), ("blk", "rep")
    )
    return (feature_grad, self_grad, neigh_grad, bias_grad)


def solution(mesh):
    return jax.shard_map(
        on_device,
        mesh=mesh,
        in_specs=(
            P(("parts", "blk", "rep"), None),
            P(("parts", "blk", "rep"), None),
            P(("parts", "blk", "rep"), None),
            P(),
            P(),
            P(),
            P(("parts", "blk"), "rep", None, None, None, None),
            P(("parts", "blk"), "rep", None, None, None),
            P(("parts", "blk"), "rep", None),
        ),
        out_specs=(
            P(("parts", "blk", "rep"), None),
            P("parts", None),
            P("parts", None),
            P("parts"),
        ),
        check_vma=False,
    )
```

profile of v0, /device:TPU:1, one launch (start us, length us, event | category | flops | bytes accessed | tf_op | source)
XLA Modules:
  0.0 115.3 jit_solution(11368677273185112621)
XLA Ops:
  7.3 1.5 %fusion.34 = f32[256,256]{1,0:T(8,128)S(1)} fusion(f32[256,128]{1,0:T(8,128)} %param.13, f32[128,256]{1,0:T(8,128)} %param.16), kind=kOutput, calls=%fused_computation.55 | convolution fusion | flops 100663296 | bytes 524288 | tf_op jit(solution)/shard_map/dot_general | solution.py:42
  8.7 1.4 %fusion.33 = (f32[256]{0:T(256)S(1)}, f32[256,256]{1,0:T(8,128)S(1)}) fusion(f32[256,256]{1,0:T(8,128)} %param.15, f32[256]{0:T(256)} %param.18, f32[256,256]{1,0:T(8,128)S(1)} %fusion.34, f32[256,128]{1,0:T(8,128)S(1)} %copy-done, f32[128,256]{1,0:T(8,128)} %param.17), kind=kOutput, calls=%fused_computation.54 | convolution fusion | flops 101383936 | bytes 1050624 | tf_op jit(solution)/shard_map/dot_general | solution.py:47
  10.2 1.3 %convolution_bitcast_fusion = f32[128,256]{0,1:T(8,128)} fusion(f32[256,256]{1,0:T(8,128)S(1)} %get-tuple-element.229, f32[256,128]{1,0:T(8,128)S(1)} %copy-done), kind=kOutput, calls=%fused_computation.27 | convolution fusion | flops 100663296 | bytes 524288 | tf_op jit(solution)/shard_map/dot_general | solution.py:86
  11.4 1.2 %convolution_bitcast_fusion.1 = f32[128,256]{0,1:T(8,128)} fusion(f32[256,256]{1,0:T(8,128)S(1)} %get-tuple-element.229, f32[256,128]{1,0:T(8,128)S(1)} %copy-done.2), kind=kOutput, calls=%fused_computation.28 | convolution fusion | flops 100663296 | bytes 524288 | tf_op jit(solution)/shard_map/dot_general | solution.py:83
  13.2 15.8 %all_gather.3 = f32[1024,128]{1,0:T(8,128)S(1)} all-gather(f32[256,128]{1,0:T(8,128)S(1)} %fusion.35), channel_id=1, replica_groups=mesh['parts'=2,'blk'=4,'rep'=4] {'rep'}, dimensions={0}, use_global_device_ids=true | all-gather | bytes 655360 | tf_op jit(solution)/shard_map/all_gather | solution.py:60
  29.6 0.6 iota_compare_fusion.1
  30.2 0.6 gather_fusion.1
  30.8 2.3 %fusion.19 = f32[10,128,128]{2,1,0:T(8,128)S(1)} fusion(f32[10,128,128]{2,1,0:T(8,128)S(1)} %gather_fusion.1, f32[1,1,4,10,128,128]{5,4,3,2,1,0:T(8,128)} %param.19, s32[]{:T(128)S(6)} %select_n.52, pred[10]{0:T(512)(128)(4,1)S(1)} %get-tuple-element.226), kind=kOutput, calls=%fused_computation.32 | convolution fusion | flops 251822080 | bytes 1966094 | tf_op jit(solution)/shard_map/tab,taf->tbf/dot_general | solution.py:21
  33.2 0.8 fusion.17
  34.0 32.7 %psum.23 = f32[256]{0:T(256)} all-reduce(f32[256]{0:T(256)S(1)} %get-tuple-element.228), channel_id=1, replica_groups=mesh['parts'=2,'blk'=4,'rep'=4] {'blk','rep'}, use_global_device_ids=true, to_apply=%region_5.7 | all-reduce | flops 256 | bytes 2048 | tf_op jit(solution)/shard_map/psum | solution.py:90
  66.7 18.8 %while.15 = (s32[]{:T(128)}, f32[256,128]{1,0:T(8,128)S(1)}, s32[]{:T(128)}, s32[4,10,2]{1,2,0:T(2,128)S(1)}, s32[4]{0:T(128)S(1)}, /*index=5*/f32[4,10,128,128]...) while((s32[]{:T(128)}, f32[256,128]{1,0:T(8,128)S(1)}, ...), condition=%wide.region_1.3_spmd, body=%wide.region_0.2_spmd.sunk | while | flops 255788160 | bytes 5247784 | solution.py:78
  66.7 2.8 %collective-permute-start = (f32[256,128]{1,0:T(8,128)S(1)}, f32[256,128]{1,0:T(8,128)S(1)}, u32[]{:S(2)}, u32[]{:S(2)}) collective-permute-start(f32[256,128]{1,0:T(8,128)S(1)} %get-tuple-element.289), channel_id=1, source_target_pairs={{12,0},{0,4},{4,8},{8,12},{13,1},{1,5},{5,9},{9,13},{14,2},{2,6},{... | collective-permute-start | bytes 393224 | tf_op jit(solution)/shard_map/while/body/eval_jaxpr/ppermute | solution.py:15
  69.5 0.6 dynamic_slice.61
  70.1 0.6 iota_compare_fusion.3
  70.8 0.6 gather_fusion
  71.4 2.3 %fusion.58 = f32[10,128,128]{2,1,0:T(8,128)S(1)} fusion(f32[10,128,128]{2,1,0:T(8,128)S(1)} %gather_fusion, f32[4,10,128,128]{3,2,1,0:T(8,128)} %get-tuple-element.304, s32[]{:T(128)S(6)} %select_n.72, pred[10]{0:T(512)(128)(4,1)S(1)} %get-tuple-element.276), kind=kOutput, calls=%fused_computation.4.clone.1 | convolution fusion | flops 251822080 | bytes 1966094 | tf_op jit(solution)/shard_map/while/body/eval_jaxpr/tab,taf->tbf/dot_general | solution.py:21
  73.7 0.8 fusion.59
  74.7 0.6 dynamic_slice.61
  75.3 0.6 iota_compare_fusion.3
  76.0 0.6 gather_fusion
  76.6 2.3 %fusion.58 = f32[10,128,128]{2,1,0:T(8,128)S(1)} fusion(f32[10,128,128]{2,1,0:T(8,128)S(1)} %gather_fusion, f32[4,10,128,128]{3,2,1,0:T(8,128)} %get-tuple-element.304, s32[]{:T(128)S(6)} %select_n.72, pred[10]{0:T(512)(128)(4,1)S(1)} %get-tuple-element.276), kind=kOutput, calls=%fused_computation.4.clone.1 | convolution fusion | flops 251822080 | bytes 1966094 | tf_op jit(solution)/shard_map/while/body/eval_jaxpr/tab,taf->tbf/dot_general | solution.py:21
  78.9 0.8 fusion.59
  79.8 0.7 collective-permute-start
  80.5 0.6 dynamic_slice.61
  81.1 0.6 iota_compare_fusion.3
  81.7 0.6 gather_fusion
  82.3 2.3 %fusion.58 = f32[10,128,128]{2,1,0:T(8,128)S(1)} fusion(f32[10,128,128]{2,1,0:T(8,128)S(1)} %gather_fusion, f32[4,10,128,128]{3,2,1,0:T(8,128)} %get-tuple-element.304, s32[]{:T(128)S(6)} %select_n.72, pred[10]{0:T(512)(128)(4,1)S(1)} %get-tuple-element.276), kind=kOutput, calls=%fused_computation.4.clone.1 | convolution fusion | flops 251822080 | bytes 1966094 | tf_op jit(solution)/shard_map/while/body/eval_jaxpr/tab,taf->tbf/dot_general | solution.py:21
  84.6 0.8 fusion.59
  85.5 1.0 convolution_add_fusion.1
  86.5 18.6 %all-reduce.3.cloned.1.call-done = (f32[128,256]{0,1:T(8,128)}, f32[128,256]{0,1:T(8,128)}) async-done(((f32[128,256]{0,1:T(8,128)}, f32[128,256]{0,1:T(8,128)}), (f32[128,256]{0,1:T(8,128)}, f32[128,256]{0,1:T(8,128)})) %all-reduce.3.cloned.1.call-update) | async-done | bytes 262160 | tf_op jit(solution)/shard_map/psum | solution.py:90
  105.1 1.7 %copy.21 = f32[128,256]{1,0:T(8,128)} copy(f32[128,256]{0,1:T(8,128)} %get-tuple-element.222) | data formatting | bytes 262144
  106.8 1.7 %copy.22 = f32[128,256]{1,0:T(8,128)} copy(f32[128,256]{0,1:T(8,128)} %get-tuple-element.223) | data formatting | bytes 262144
  (43 shorter events, 1.3 us)
Async XLA Ops:
  7.2 1.6 %copy-start = (f32[256,128]{1,0:T(8,128)S(1)}, f32[256,128]{1,0:T(8,128)}, u32[]{:S(2)}) copy-start(f32[256,128]{1,0:T(8,128)} %param.14) | copy-start | bytes 393220
  7.2 4.3 %copy-start.2 = (f32[256,128]{1,0:T(8,128)S(1)}, f32[256,128]{1,0:T(8,128)}, u32[]{:S(2)}) copy-start(f32[256,128]{1,0:T(8,128)} %param.13) | copy-start | bytes 393220
  7.2 5.5 %copy-start.3 = (f32[128,256]{1,0:T(8,128)S(1)}, f32[128,256]{1,0:T(8,128)}, u32[]{:S(2)}) copy-start(f32[128,256]{1,0:T(8,128)} %param.17) | copy-start | bytes 393220
  7.2 5.9 %copy-start.4 = (s32[1,1,4,10,2]{3,4,2,1,0:T(2,128)S(1)}, s32[1,1,4,10,2]{3,4,2,1,0:T(2,128)}, u32[]{:S(2)}) copy-start(s32[1,1,4,10,2]{3,4,2,1,0:T(2,128)} %param.20) | copy-start | bytes 964
  7.2 21.8 %copy-start.5 = (s32[1,1,4]{2,1,0:T(1,128)S(1)}, s32[1,1,4]{2,1,0:T(1,128)}, u32[]{:S(2)}) copy-start(s32[1,1,4]{2,1,0:T(1,128)} %param.21) | copy-start | bytes 52
  7.2 97.9 %all-reduce.3.cloned.1.call-start = ((), (), s32[]{:S(2)}) async-start(), calls=%async_computation | async-start | bytes 524288 | tf_op jit(solution)/shard_map/psum | solution.py:90
  66.7 18.8 %copy-start.1 = (f32[128,256]{1,0:T(8,128)S(1)}, f32[128,256]{1,0:T(8,128)}, u32[]{:S(2)}) copy-start(f32[128,256]{1,0:T(8,128)} %param.16) | copy-start | bytes 393220
  66.7 7.8 %collective-permute-start = (f32[256,128]{1,0:T(8,128)S(1)}, f32[256,128]{1,0:T(8,128)S(1)}, u32[]{:S(2)}, u32[]{:S(2)}) collective-permute-start(f32[256,128]{1,0:T(8,128)S(1)} %get-tuple-element.289), channel_id=1, source_target_pairs={{12,0},{0,4},{4,8},{8,12},{13,1},{1,5},{5,9},{9,13},{14,2},{2,6},{... | collective-permute-start | bytes 393224 | tf_op jit(solution)/shard_map/while/body/eval_jaxpr/ppermute | solution.py:15
  74.6 5.1 %collective-permute-start = (f32[256,128]{1,0:T(8,128)S(1)}, f32[256,128]{1,0:T(8,128)S(1)}, u32[]{:S(2)}, u32[]{:S(2)}) collective-permute-start(f32[256,128]{1,0:T(8,128)S(1)} %get-tuple-element.289), channel_id=1, source_target_pairs={{12,0},{0,4},{4,8},{8,12},{13,1},{1,5},{5,9},{9,13},{14,2},{2,6},{... | collective-permute-start | bytes 393224 | tf_op jit(solution)/shard_map/while/body/eval_jaxpr/ppermute | solution.py:15
  79.8 5.7 %collective-permute-start = (f32[256,128]{1,0:T(8,128)S(1)}, f32[256,128]{1,0:T(8,128)S(1)}, u32[]{:S(2)}, u32[]{:S(2)}) collective-permute-start(f32[256,128]{1,0:T(8,128)S(1)} %get-tuple-element.289), channel_id=1, source_target_pairs={{12,0},{0,4},{4,8},{8,12},{13,1},{1,5},{5,9},{9,13},{14,2},{2,6},{... | collective-permute-start | bytes 393224 | tf_op jit(solution)/shard_map/while/body/eval_jaxpr/ppermute | solution.py:15
Sparse Core Ops, SparseCore 0:
  12.8 92.2 all-reduce.2
where the time goes:
time: 116 us; the launch traced here: 115 us
  blocking collectives  48.5 us (42%)
  matrix products  19.3 us (17%)
  waiting for transfers between devices  18.6 us (16%)
  between operations  14.2 us (12%)
  local copies, waits for them, and re-layouts  8.17 us (7%)
  starting transfers between devices  3.54 us (3%)
  other arithmetic  2.64 us (2%)
    psum x1, blocking collectives, on_device(): lax.psum((self_local, neighbour_part, bias_local), ('blk', 'rep'))  32.7 us
    psum x1, waiting for transfers between devices, on_device(): lax.psum((self_local, neighbour_part, bias_local), ('blk', 'rep'))  18.6 us
    all_gather x1, blocking collectives, on_device(): block_grad = lax.all_gather(d_agg, 'rep', axis=0, tiled=True)  15.8 us
    dot_general x4, matrix products, block_terms(): jnp.einsum('tab,taf->tbf', tile_block, chosen_tiles, precision=top_precis...  9.34 us
    ppermute x3, starting transfers between devices, from_behind(): return lax.ppermute(block, axis, route)  3.5 us
    unnamed x14, local copies, waits for them, and re-layouts  3.35 us
    dot_general x4, matrix products, block_terms(): jnp.einsum('ip,iwe->pwe', select_tile, tile_products, precision=top_preci...  3.18 us
    lt x4, other arithmetic, block_terms(): live = jnp.arange(TCAP, dtype=jnp.int32) < tile_count  2.53 us
  transfers between devices with their start and end apart: 4, of which 1 were waited for; matrix products, arithmetic and copies ran while one was open for 19% of the time, Pallas kernels for 0%

commit v1 on v0

v1 whole, which is shorter than its diff:
```python
import functools

import jax
import jax.numpy as jnp
from jax import lax
from jax.experimental import pallas as pl
from jax.experimental.pallas import tpu as pltpu
from jax.sharding import PartitionSpec as P

F = 128
H = 256
TILE = 128
TR = 2
TCAP = 10
MESH = pl.DeviceIdType.MESH
NN = (((1,), (0,)), ((), ()))
NT = (((1,), (1,)), ((), ()))


def split(x):
    hi = x.astype(jnp.bfloat16)
    return hi, (x - hi.astype(jnp.float32)).astype(jnp.bfloat16)


def dot3(a, b, dims):
    def one(p, q):
        return lax.dot_general(p, q, dims, preferred_element_type=jnp.float32)

    return one(a[0], b[0]) + (one(a[0], b[1]) + one(a[1], b[0]))


def kernel(
    blks, reps,
    feat, nm, og, ws, wn, bias, coords, counts, tiles,
    fg_out, sg_out, ng_out, bg_out,
    tv, th, tl, gather, gh, gl, lhs_h, lhs_l, dself,
    wbuf, wrecv, acc, tot_in, back, total,
    part, pair, sib_recv, far_recv,
    tile_sem, gs_sem, gr_sem, ws_sem, wr_sem, chain_s, chain_r, ts_sem, tr_sem,
    sib_s, sib_r, far_s, far_r,
):
    b = lax.axis_index("blk")
    z = lax.axis_index("rep")
    chips = blks // 2
    chip, core = b // 2, b % 2
    rows = 2 * F // blks
    has_left, has_right = z > 0, z < reps - 1

    def remote(src, dst, ssem, rsem, **where):
        return pltpu.make_async_remote_copy(
            src_ref=src, dst_ref=dst, send_sem=ssem, recv_sem=rsem,
            device_id=where, device_id_type=MESH,
        )

    barrier = pltpu.get_barrier_semaphore()
    for d in range(1, blks):
        pl.semaphore_signal(
            barrier, inc=1, device_id={"blk": (b + d) % blks}, device_id_type=MESH
        )

    @pl.when(has_left)
    def _():
        pl.semaphore_signal(barrier, inc=1, device_id={"rep": z - 1}, device_id_type=MESH)

    @pl.when(has_right)
    def _():
        pl.semaphore_signal(barrier, inc=1, device_id={"rep": z + 1}, device_id_type=MESH)

    tile_copies = [
        pltpu.make_async_copy(tiles.at[j], tv.at[j], tile_sem.at[j]) for j in range(blks)
    ]
    for c in tile_copies:
        c.start()

    x = jnp.concatenate([feat[...], nm[...]], axis=1)
    w = split(jnp.concatenate([ws[...], wn[...]], axis=0))
    pre = dot3(split(x), w, NN) + bias[...]
    sig = 1.0 / (1.0 + jnp.exp(-pre))
    d_pre = og[...] * sig * (1.0 + pre * (1.0 - sig))
    d_split = split(d_pre)
    dx = dot3(d_split, w, NT)
    for i in range(TR):
        gather[TR * z + i] = dx[i * TILE : (i + 1) * TILE, F:].T

    ends = jnp.where((z == 0) | (z == reps - 1), 1, 2)
    pl.semaphore_wait(barrier, blks - 1 + ends)

    def gather_copy(direction, step, i):
        block = z - step if direction == 0 else z + step
        to = z + 1 if direction == 0 else z - 1
        slot = gather.at[TR * block + i]
        return remote(
            slot, slot, gs_sem.at[direction, step, i], gr_sem.at[direction, step, i], rep=to
        )

    def sends(direction, step):
        if direction == 0:
            return (z >= step) & has_right
        return (z + step < reps) & has_left

    def receives(direction, step):
        if direction == 0:
            return z - 1 >= step
        return z + 1 + step < reps

    def split_block(slot):
        hi, lo = split(gather[slot])
        gh[slot] = hi
        gl[slot] = lo

    def gather_step(step):
        for i in range(TR):
            for direction in range(2):

                @pl.when(receives(direction, step))
                def _():
                    block = z - 1 - step if direction == 0 else z + 1 + step
                    slot = gather.at[TR * block + i]
                    remote(
                        slot, slot,
                        gs_sem.at[direction, step, i], gr_sem.at[direction, step, i],
                        rep=z - 1 if direction == 0 else z + 1,
                    ).wait_recv()
                    if step + 1 < reps - 1:

                        @pl.when(sends(direction, step + 1))
                        def _():
                            gather_copy(direction, step + 1, i).start()

        for i in range(TR):
            for direction in range(2):

                @pl.when(receives(direction, step))
                def _():
                    block = z - 1 - step if direction == 0 else z + 1 + step
                    split_block(TR * block + i)

    for i in range(TR):
        for direction in range(2):

            @pl.when(sends(direction, 0))
            def _():
                gather_copy(direction, 0, i).start()

    grad_w = dot3(split(x.T), d_split, NN)
    grad_b = jnp.broadcast_to(jnp.sum(d_pre, axis=0, keepdims=True), (8, H))
    for j in range(blks):
        wbuf[j, :rows] = grad_w[j * rows : (j + 1) * rows]
        wbuf[j, rows:] = grad_b
    w_copies = []
    for d in range(1, blks):
        to = (b + d) % blks
        w_copies.append(
            remote(wbuf.at[to], wrecv.at[d - 1], ws_sem.at[d - 1], wr_sem.at[d - 1], blk=to)
        )
    for c in w_copies:
        c.start()

    dself[...] = dx[:, :F]
    for i in range(TR):
        split_block(TR * z + i)

    def split_tiles(j):
        tile_copies[j].wait()
        hi, lo = split(tv[j])
        th[j] = hi
        tl[j] = lo

    gather_step(0)
    for j in range(blks // 2):
        split_tiles(j)

    for c in w_copies:
        c.wait_recv()
    own = wbuf[b]
    for d in range(1, blks):
        own = own + wrecv[d - 1]
    acc[...] = own
    left_half = z < reps // 2
    inner = jnp.where(left_half, z + 1, z - 1)
    outer = jnp.where(left_half, z - 1, z + 1)
    at_end = (z == 0) | (z == reps - 1)
    at_middle = (z == reps // 2 - 1) | (z == reps // 2)
    to_inner = remote(acc, tot_in, chain_s.at[0], chain_r.at[0], rep=inner)
    to_middle = remote(acc, back, chain_s.at[1], chain_r.at[1], rep=inner)
    to_outer = remote(total.at[b], back, chain_s.at[2], chain_r.at[1], rep=outer)

    @pl.when(jnp.logical_not(at_end))
    def _():
        remote(acc, tot_in, chain_s.at[0], chain_r.at[0], rep=outer).wait_recv()
        acc[...] = acc[...] + tot_in[...]

    @pl.when(jnp.logical_not(at_middle))
    def _():
        to_inner.start()

    @pl.when(at_middle)
    def _():
        to_middle.start()

    for step in range(1, reps - 1):
        gather_step(step)
        if step == 1:
            for j in range(blks // 2, blks):
                split_tiles(j)

    to_middle.wait_recv()

    @pl.when(at_middle)
    def _():
        total[b] = acc[...] + back[...]

    @pl.when(jnp.logical_not(at_middle))
    def _():
        total[b] = back[...]

    @pl.when(jnp.logical_not(at_end))
    def _():
        to_outer.start()

    t_copies = []
    for d in range(1, blks):
        t_copies.append(
            remote(total.at[b], total.at[b], ts_sem.at[d - 1], tr_sem.at[d - 1], blk=(b + d) % blks)
        )
    for c in t_copies:
        c.start()

    def product(j):
        for t in range(TCAP):
            row = coords[(j * TCAP + t) * 2]
            col = coords[(j * TCAP + t) * 2 + 1]
            live = (t < counts[j]).astype(jnp.int32)
            hi, lo = gh[row], gl[row]
            for c in range(TR):
                on = (live * (col == c).astype(jnp.int32)).astype(jnp.float32)
                mask = jnp.full((1, TILE), on, jnp.float32).astype(jnp.bfloat16)
                lhs_h[c * F : (c + 1) * F, t * TILE : (t + 1) * TILE] = hi * mask
                lhs_l[c * F : (c + 1) * F, t * TILE : (t + 1) * TILE] = lo * mask
        return dot3((lhs_h[...], lhs_l[...]), (th[j], tl[j]), NN)

    def to_sibling(d):
        return remote(
            part.at[d], sib_recv.at[d], sib_s.at[d], sib_r.at[d], blk=2 * chip + (1 - core)
        )

    def to_far(d):
        return remote(
            pair.at[d - 1], far_recv.at[d - 1], far_s.at[d - 1], far_r.at[d - 1],
            blk=2 * ((chip + d) % chips) + core,
        )

    for d in list(range(1, chips)) + [0]:
        at = (chip + d) % chips
        part[d] = product(2 * at + (1 - core))
        to_sibling(d).start()
        mine = product(2 * at + core)
        to_sibling(d).wait_recv()
        mine = mine + sib_recv[d]
        if d > 0:
            pair[d - 1] = mine
            to_far(d).start()

    for c in t_copies:
        c.wait_recv()
    half = blks // 2
    for j in range(half):
        sg_out[j * rows : (j + 1) * rows] = total[j, :rows]
        ng_out[j * rows : (j + 1) * rows] = total[half + j, :rows]
    bg_out[...] = total[0, rows : rows + 1]

    for d in range(1, chips):
        to_far(d).wait_recv()
        mine = mine + far_recv[d - 1]
    for i in range(TR):
        fg_out[i * TILE : (i + 1) * TILE] = (
            dself[i * TILE : (i + 1) * TILE] + mine[i * F : (i + 1) * F].T
        )

    for step in range(reps - 1):
        for i in range(TR):
            for direction in range(2):

                @pl.when(sends(direction, step))
                def _():
                    gather_copy(direction, step, i).wait_send()

    for c in w_copies + t_copies:
        c.wait_send()

    @pl.when(jnp.logical_not(at_middle))
    def _():
        to_inner.wait_send()

    @pl.when(at_middle)
    def _():
        to_middle.wait_send()

    @pl.when(jnp.logical_not(at_end))
    def _():
        to_outer.wait_send()

    for d in range(chips):
        to_sibling(d).wait_send()
    for d in range(1, chips):
        to_far(d).wait_send()


def on_device(blks, reps, features, neighbour_mean, out_grad, self_weight, neigh_weight, bias,
              tile_values, tile_coords, tile_counts):
    chips = blks // 2
    rows = 2 * F // blks
    nodes = TR * TILE
    f32, bf16 = jnp.float32, jnp.bfloat16
    vmem = pl.BlockSpec(memory_space=pltpu.VMEM)
    smem = pl.BlockSpec(memory_space=pltpu.SMEM)
    dma = pltpu.SemaphoreType.DMA
    chunk = (rows + 8, H)
    feature_grad, self_grad, neigh_grad, bias_grad = pl.pallas_call(
        functools.partial(kernel, blks, reps),
        out_shape=(
            jax.ShapeDtypeStruct((nodes, F), f32),
            jax.ShapeDtypeStruct((F, H), f32),
            jax.ShapeDtypeStruct((F, H), f32),
            jax.ShapeDtypeStruct((1, H), f32),
        ),
        in_specs=[vmem] * 6 + [smem, smem, pl.BlockSpec(memory_space=pl.ANY)],
        out_specs=(vmem,) * 4,
        scratch_shapes=[
            pltpu.VMEM((blks, TCAP * TILE, TILE), f32),
            pltpu.VMEM((blks, TCAP * TILE, TILE), bf16),
            pltpu.VMEM((blks, TCAP * TILE, TILE), bf16),
            pltpu.VMEM((reps * TR, F, TILE), f32),
            pltpu.VMEM((reps * TR, F, TILE), bf16),
            pltpu.VMEM((reps * TR, F, TILE), bf16),
            pltpu.VMEM((TR * F, TCAP * TILE), bf16),
            pltpu.VMEM((TR * F, TCAP * TILE), bf16),
            pltpu.VMEM((nodes, F), f32),
            pltpu.VMEM((blks,) + chunk, f32),
            pltpu.VMEM((blks - 1,) + chunk, f32),
            pltpu.VMEM(chunk, f32),
            pltpu.VMEM(chunk, f32),
            pltpu.VMEM(chunk, f32),
            pltpu.VMEM((blks,) + chunk, f32),
            pltpu.VMEM((chips, TR * F, TILE), f32),
            pltpu.VMEM((chips - 1, TR * F, TILE), f32),
            pltpu.VMEM((chips, TR * F, TILE), f32),
            pltpu.VMEM((chips - 1, TR * F, TILE), f32),
            dma((blks,)),
            dma((2, reps - 1, TR)), dma((2, reps - 1, TR)),
            dma((blks - 1,)), dma((blks - 1,)),
            dma((3,)), dma((2,)),
            dma((blks - 1,)), dma((blks - 1,)),
            dma((chips,)), dma((chips,)),
            dma((chips - 1,)), dma((chips - 1,)),
        ],
        compiler_params=pltpu.CompilerParams(
            collective_id=0, has_side_effects=True, vmem_limit_bytes=56 * 2**20
        ),
    )(
        features, neighbour_mean, out_grad, self_weight, neigh_weight, bias.reshape(1, H),
        tile_coords.reshape(-1), tile_counts.reshape(-1),
        tile_values.reshape(blks, TCAP * TILE, TILE),
    )
    return feature_grad, self_grad, neigh_grad, bias_grad.reshape(H)


def solution(mesh):
    return jax.shard_map(
        functools.partial(on_device, mesh.shape["blk"], mesh.shape["rep"]),
        mesh=mesh,
        in_specs=(
            P(("parts", "blk", "rep"), None),
            P(("parts", "blk", "rep"), None),
            P(("parts", "blk", "rep"), None),
            P(),
            P(),
            P(),
            P(("parts", "blk"), "rep", None, None, None, None),
            P(("parts", "blk"), "rep", None, None, None),
            P(("parts", "blk"), "rep", None),
        ),
        out_specs=(
            P(("parts", "blk", "rep"), None),
            P("parts", None),
            P("parts", None),
            P("parts"),
        ),
        check_vma=False,
    )
```

time: 116 us -> 38.1 us (0.33)
  blocking collectives: 48.5 us -> 0 us
  Pallas kernels: 0 us -> 29.5 us
  matrix products: 19.3 us -> 0 us
  waiting for transfers between devices: 18.6 us -> 0 us
  between operations: 14.2 us -> 0.64 us
  starting transfers between devices: 3.54 us -> 0 us
  other arithmetic: 2.64 us -> 0 us
    psum x1 -> x0, blocking collectives: 32.7 us -> none  [on_device(): lax.psum((self_local, neighbour_part, bias_local), ('blk', 'rep'))]
    pallas_call x0 -> x1, Pallas kernels: none -> 29.5 us  [on_device(): pl.pallas_call(functools.partial(kernel, blks, reps), out_shape=(jax.Shap...]
    dot_general x14 -> x0, matrix products: 19.3 us -> none  [the longest x4 9.34 us: block_terms(): jnp.einsum('tab,taf->tbf', tile_block, chosen_tiles, precision=top_precis...]
    psum x1 -> x0, waiting for transfers between devices: 18.6 us -> none  [on_device(): lax.psum((self_local, neighbour_part, bias_local), ('blk', 'rep'))]
    all_gather x1 -> x0, blocking collectives: 15.8 us -> none  [on_device(): block_grad = lax.all_gather(d_agg, 'rep', axis=0, tiled=True)]
    ppermute x3 -> x0, starting transfers between devices: 3.5 us -> none  [from_behind(): return lax.ppermute(block, axis, route)]
    unnamed x14 -> x5, local copies, waits for them, and re-layouts: 3.35 us -> 6.69 us
    lt x4 -> x0, other arithmetic: 2.53 us -> none  [block_terms(): live = jnp.arange(TCAP, dtype=jnp.int32) < tile_count]
  transfers between devices with their start and end apart: 4 -> 0, of which waited for: 1 -> 0; matrix products, arithmetic and copies ran while one was open for 19% -> 0% of each run, Pallas kernels for 0% -> 0%
where the time goes in v1:
time: 38.1 us; the launch traced here: 37.4 us
  Pallas kernels  29.5 us (77%)
  local copies, waits for them, and re-layouts  7.32 us (19%)
  between operations  0.64 us (2%)
    pallas_call x1, Pallas kernels, on_device(): pl.pallas_call(functools.partial(kernel, blks, reps), out_shape=(jax.Shap...  29.5 us
    unnamed x5, local copies, waits for them, and re-layouts  6.69 us

profile of v1, /device:TPU:1, one launch (start us, length us, event | category | flops | bytes accessed | tf_op | source)
XLA Modules:
  0.0 37.4 jit_solution(8343998065306449377)
XLA Ops:
  0.6 0.8 %copy.14 = s32[1,1,4,10,2]{4,3,2,1,0:T(8,128)S(1)} copy(s32[1,1,4,10,2]{3,4,2,1,0:T(2,128)} %param.16) | data formatting | bytes 640 | tf_op args[7]
  1.4 0.6 %reshape.24.coords = s32[80]{0:T(128)} reshape(s32[1,1,4,10,2]{4,3,2,1,0:T(8,128)S(1)} %copy.14) | data formatting | bytes 640 | tf_op jit(solution)/shard_map/reshape | solution.py:362
  2.1 29.5 %shard_map.120 = (f32[256,128]{1,0:T(8,128)}, f32[128,256]{1,0:T(8,128)}, f32[128,256]{1,0:T(8,128)}, f32[1,256]{1,0:T(1,128)}) custom-call(f32[256,128]{1,0:T(8,128)} %feat.1, f32[256,128]{1,0:T(8,128)} %nm.1, f32[256,256]{1,0:T(8,128)} %og.1, f32[128,256]{1,0:T(8,128)} %ws.1, f32[128,256]{1,0:T(8,128)} %wn.1, f32[1,256]{1,0:T(1,128)} %bitcast.5, ...), custom_call_target="tpu_custom_call" | custom-call | tf_op jit(solution)/shard_map/pallas_call | solution.py:319
  31.5 1.6 %copy.19 = f32[256,128]{1,0:T(8,128)} copy(f32[256,128]{1,0:T(8,128)} %get-tuple-element.16) | data formatting | bytes 262144
  33.1 1.6 %copy.20 = f32[128,256]{1,0:T(8,128)} copy(f32[128,256]{1,0:T(8,128)} %get-tuple-element.17) | data formatting | bytes 262144
  34.7 1.6 %copy.21 = f32[128,256]{1,0:T(8,128)} copy(f32[128,256]{1,0:T(8,128)} %get-tuple-element.18) | data formatting | bytes 262144
  36.2 1.2 %copy.22 = f32[256]{0:T(256)} copy(f32[256]{0:T(256)} %bitcast.6) | data formatting | bytes 2048

commit v2 on v1

--- a/solution.py
+++ b/solution.py
@@ -185,12 +185,19 @@
     to_middle = remote(acc, back, chain_s.at[1], chain_r.at[1], rep=inner)
     to_outer = remote(total.at[b], back, chain_s.at[2], chain_r.at[1], rep=outer)
 
+    @pl.when(at_end & jnp.logical_not(at_middle))
+    def _():
+        to_inner.start()
+
+    for step in range(1, reps - 2):
+        gather_step(step)
+
     @pl.when(jnp.logical_not(at_end))
     def _():
         remote(acc, tot_in, chain_s.at[0], chain_r.at[0], rep=outer).wait_recv()
         acc[...] = acc[...] + tot_in[...]
 
-    @pl.when(jnp.logical_not(at_middle))
+    @pl.when(jnp.logical_not(at_end | at_middle))
     def _():
         to_inner.start()
 
@@ -198,38 +205,43 @@
     def _():
         to_middle.start()
 
-    for step in range(1, reps - 1):
-        gather_step(step)
-        if step == 1:
-            for j in range(blks // 2, blks):
-                split_tiles(j)
-
-    to_middle.wait_recv()
+    for j in range(blks // 2, blks):
+        split_tiles(j)
+
+    sibling = 2 * chip + (1 - core)
+
+    def to_chip(d):
+        mine = total.at[b]
+        return remote(
+            mine, mine, ts_sem.at[d - 1], tr_sem.at[d - 1], blk=2 * ((chip + d) % chips) + core
+        )
+
+    def pass_on(d):
+        slot = total.at[2 * ((chip + chips - d) % chips) + core]
+        at = chips - 1 + d
+        return remote(slot, slot, ts_sem.at[at], tr_sem.at[at], blk=sibling)
+
+    def spread():
+        @pl.when(jnp.logical_not(at_end))
+        def _():
+            to_outer.start()
+
+        for d in range(1, chips):
+            to_chip(d).start()
+        pass_on(0).start()
 
     @pl.when(at_middle)
     def _():
+        to_middle.wait_recv()
         total[b] = acc[...] + back[...]
-
-    @pl.when(jnp.logical_not(at_middle))
-    def _():
-        total[b] = back[...]
-
-    @pl.when(jnp.logical_not(at_end))
-    def _():
-        to_outer.start()
-
-    t_copies = []
-    for d in range(1, blks):
-        t_copies.append(
-            remote(total.at[b], total.at[b], ts_sem.at[d - 1], tr_sem.at[d - 1], blk=(b + d) % blks)
-        )
-    for c in t_copies:
-        c.start()
+        spread()
+
+    gather_step(reps - 2)
 
     def product(j):
         for t in range(TCAP):
-            row = coords[(j * TCAP + t) * 2]
-            col = coords[(j * TCAP + t) * 2 + 1]
+            row = coords[j, 0, t]
+            col = coords[j, 1, t]
             live = (t < counts[j]).astype(jnp.int32)
             hi, lo = gh[row], gl[row]
             for c in range(TR):
@@ -241,7 +253,7 @@
 
     def to_sibling(d):
         return remote(
-            part.at[d], sib_recv.at[d], sib_s.at[d], sib_r.at[d], blk=2 * chip + (1 - core)
+            part.at[d], sib_recv.at[d], sib_s.at[d], sib_r.at[d], blk=sibling
         )
 
     def to_far(d):
@@ -250,19 +262,31 @@
             blk=2 * ((chip + d) % chips) + core,
         )
 
-    for d in list(range(1, chips)) + [0]:
+    def pair_sum(d):
         at = (chip + d) % chips
         part[d] = product(2 * at + (1 - core))
         to_sibling(d).start()
         mine = product(2 * at + core)
         to_sibling(d).wait_recv()
-        mine = mine + sib_recv[d]
-        if d > 0:
-            pair[d - 1] = mine
-            to_far(d).start()
-
-    for c in t_copies:
-        c.wait_recv()
+        return mine + sib_recv[d]
+
+    for d in range(1, chips):
+        pair[d - 1] = pair_sum(d)
+        to_far(d).start()
+
+    @pl.when(jnp.logical_not(at_middle))
+    def _():
+        to_middle.wait_recv()
+        total[b] = back[...]
+        spread()
+
+    mine = pair_sum(0)
+
+    for d in range(1, chips):
+        to_chip(d).wait_recv()
+        pass_on(d).start()
+    for d in range(chips):
+        pass_on(d).wait_recv()
     half = blks // 2
     for j in range(half):
         sg_out[j * rows : (j + 1) * rows] = total[j, :rows]
@@ -285,8 +309,12 @@
                 def _():
                     gather_copy(direction, step, i).wait_send()
 
-    for c in w_copies + t_copies:
+    for c in w_copies:
         c.wait_send()
+    for d in range(1, chips):
+        to_chip(d).wait_send()
+    for d in range(chips):
+        pass_on(d).wait_send()
 
     @pl.when(jnp.logical_not(at_middle))
     def _():
@@ -304,6 +332,11 @@
         to_sibling(d).wait_send()
     for d in range(1, chips):
         to_far(d).wait_send()
+
+
+def hand_on(*refs):
+    for source, target in zip(refs[:4], refs[4:]):
+        target[...] = source[...]
 
 
 def on_device(blks, reps, features, neighbour_mean, out_grad, self_weight, neigh_weight, bias,
@@ -359,9 +392,16 @@
         ),
     )(
         features, neighbour_mean, out_grad, self_weight, neigh_weight, bias.reshape(1, H),
-        tile_coords.reshape(-1), tile_counts.reshape(-1),
+        jnp.swapaxes(tile_coords, 3, 4).reshape(blks, 2, TCAP), tile_counts.reshape(-1),
         tile_values.reshape(blks, TCAP * TILE, TILE),
     )
+    results = (feature_grad, self_grad, neigh_grad, bias_grad)
+    feature_grad, self_grad, neigh_grad, bias_grad = pl.pallas_call(
+        hand_on,
+        out_shape=tuple(jax.ShapeDtypeStruct(a.shape, a.dtype) for a in results),
+        in_specs=[vmem] * 4,
+        out_specs=(vmem,) * 4,
+    )(*results)
     return feature_grad, self_grad, neigh_grad, bias_grad.reshape(H)
 
 

time: 38.1 us -> 30.4 us (0.80); the launches traced: 37.4 us -> 30.2 us
  local copies, waits for them, and re-layouts: 7.32 us -> 0 us
    unnamed x5 -> x0, local copies, waits for them, and re-layouts: 6.69 us -> none
    pallas_call x0 -> x1, Pallas kernels: none -> 1.79 us  [on_device(): pl.pallas_call(hand_on, out_shape=tuple((jax.ShapeDtypeStruct(a.shape, a....]
    pallas_call x1, Pallas kernels: 29.5 us -> 27.8 us  [on_device(): pl.pallas_call(functools.partial(kernel, blks, reps), out_shape=(jax.Shap...]
    reshape x1 -> x0, local copies, waits for them, and re-layouts: 0.63 us -> none  [on_device(): tile_coords.reshape(-1)]
where the time goes in v2:
time: 30.4 us; the launch traced here: 30.2 us
  Pallas kernels  29.6 us (97%)
  between operations  0.64 us (2%)
    pallas_call x1, Pallas kernels, on_device(): pl.pallas_call(functools.partial(kernel, blks, reps), out_shape=(jax.Shap...  27.8 us
    pallas_call x1, Pallas kernels, on_device(): pl.pallas_call(hand_on, out_shape=tuple((jax.ShapeDtypeStruct(a.shape, a....  1.79 us

profile of v2, /device:TPU:1, one launch (start us, length us, event | category | flops | bytes accessed | tf_op | source)
XLA Modules:
  0.0 30.2 jit_solution(12673640791567183019)
XLA Ops:
  0.6 27.8 %shard_map.120 = (f32[256,128]{1,0:T(8,128)}, f32[128,256]{1,0:T(8,128)}, f32[128,256]{1,0:T(8,128)}, f32[1,256]{1,0:T(1,128)}) custom-call(f32[256,128]{1,0:T(8,128)} %feat.1, f32[256,128]{1,0:T(8,128)} %nm.1, f32[256,256]{1,0:T(8,128)} %og.1, f32[128,256]{1,0:T(8,128)} %ws.1, f32[128,256]{1,0:T(8,128)} %wn.1, f32[1,256]{1,0:T(1,128)} %bitcast.9, ...), custom_call_target="tpu_custom_call" | custom-call | tf_op jit(solution)/shard_map/pallas_call | solution.py:352
  28.4 1.8 %shard_map.121 = (f32[256,128]{1,0:T(8,128)}, f32[128,256]{1,0:T(8,128)}, f32[128,256]{1,0:T(8,128)}, f32[1,256]{1,0:T(1,128)}) custom-call(f32[256,128]{1,0:T(8,128)} %get-tuple-element.12.refs_0_, f32[128,256]{1,0:T(8,128)} %get-tuple-element.13.refs_1_, f32[128,256]{1,0:T(8,128)} %get-tuple-element.14.refs_2_, f32[1,256]{1,0:T(1,128)} %get-tuple-element.15.refs_3_), custom_call_target="tpu_custom_call" | custom-call | tf_op jit(solution)/shard_map/pallas_call | solution.py:399

commit v3 on v2

--- a/solution.py
+++ b/solution.py
@@ -181,60 +181,68 @@
     outer = jnp.where(left_half, z - 1, z + 1)
     at_end = (z == 0) | (z == reps - 1)
     at_middle = (z == reps // 2 - 1) | (z == reps // 2)
-    to_inner = remote(acc, tot_in, chain_s.at[0], chain_r.at[0], rep=inner)
-    to_middle = remote(acc, back, chain_s.at[1], chain_r.at[1], rep=inner)
-    to_outer = remote(total.at[b], back, chain_s.at[2], chain_r.at[1], rep=outer)
+    first = (rows + 8) // 16 * 8
+    pieces = [pl.ds(0, first), pl.ds(first, rows + 8 - first)]
+
+    def to_inner(h):
+        return remote(
+            acc.at[pieces[h]], tot_in.at[pieces[h]], chain_s.at[0, h], chain_r.at[0, h], rep=inner
+        )
+
+    def from_outer(h):
+        return remote(
+            acc.at[pieces[h]], tot_in.at[pieces[h]], chain_s.at[0, h], chain_r.at[0, h], rep=outer
+        )
+
+    def to_middle(h):
+        return remote(
+            acc.at[pieces[h]], back.at[pieces[h]], chain_s.at[1, h], chain_r.at[1, h], rep=inner
+        )
+
+    def to_outer(h):
+        return remote(
+            total.at[b, pieces[h]], back.at[pieces[h]], chain_s.at[2, h], chain_r.at[1, h], rep=outer
+        )
 
     @pl.when(at_end & jnp.logical_not(at_middle))
     def _():
-        to_inner.start()
+        for h in range(2):
+            to_inner(h).start()
 
     for step in range(1, reps - 2):
         gather_step(step)
 
-    @pl.when(jnp.logical_not(at_end))
-    def _():
-        remote(acc, tot_in, chain_s.at[0], chain_r.at[0], rep=outer).wait_recv()
-        acc[...] = acc[...] + tot_in[...]
-
-    @pl.when(jnp.logical_not(at_end | at_middle))
-    def _():
-        to_inner.start()
-
-    @pl.when(at_middle)
-    def _():
-        to_middle.start()
-
     for j in range(blks // 2, blks):
         split_tiles(j)
 
+    for h in range(2):
+
+        @pl.when(jnp.logical_not(at_end))
+        def _():
+            from_outer(h).wait_recv()
+            acc[pieces[h]] = acc[pieces[h]] + tot_in[pieces[h]]
+
+        @pl.when(jnp.logical_not(at_end | at_middle))
+        def _():
+            to_inner(h).start()
+
+        @pl.when(at_middle)
+        def _():
+            to_middle(h).start()
+
     sibling = 2 * chip + (1 - core)
 
-    def to_chip(d):
-        mine = total.at[b]
-        return remote(
-            mine, mine, ts_sem.at[d - 1], tr_sem.at[d - 1], blk=2 * ((chip + d) % chips) + core
-        )
-
-    def pass_on(d):
-        slot = total.at[2 * ((chip + chips - d) % chips) + core]
+    def to_chip(d, h):
+        mine = total.at[b, pieces[h]]
+        return remote(
+            mine, mine, ts_sem.at[d - 1, h], tr_sem.at[d - 1, h],
+            blk=2 * ((chip + d) % chips) + core,
+        )
+
+    def pass_on(d, h):
+        slot = total.at[2 * ((chip + chips - d) % chips) + core, pieces[h]]
         at = chips - 1 + d
-        return remote(slot, slot, ts_sem.at[at], tr_sem.at[at], blk=sibling)
-
-    def spread():
-        @pl.when(jnp.logical_not(at_end))
-        def _():
-            to_outer.start()
-
-        for d in range(1, chips):
-            to_chip(d).start()
-        pass_on(0).start()
-
-    @pl.when(at_middle)
-    def _():
-        to_middle.wait_recv()
-        total[b] = acc[...] + back[...]
-        spread()
+        return remote(slot, slot, ts_sem.at[at, h], tr_sem.at[at, h], blk=sibling)
 
     gather_step(reps - 2)
 
@@ -274,19 +282,34 @@
         pair[d - 1] = pair_sum(d)
         to_far(d).start()
 
-    @pl.when(jnp.logical_not(at_middle))
-    def _():
-        to_middle.wait_recv()
-        total[b] = back[...]
-        spread()
+    for h in range(2):
+        to_middle(h).wait_recv()
+
+        @pl.when(at_middle)
+        def _():
+            total[b, pieces[h]] = acc[pieces[h]] + back[pieces[h]]
+
+        @pl.when(jnp.logical_not(at_middle))
+        def _():
+            total[b, pieces[h]] = back[pieces[h]]
+
+        @pl.when(jnp.logical_not(at_end))
+        def _():
+            to_outer(h).start()
+
+        for d in range(1, chips):
+            to_chip(d, h).start()
+        pass_on(0, h).start()
 
     mine = pair_sum(0)
 
     for d in range(1, chips):
-        to_chip(d).wait_recv()
-        pass_on(d).start()
+        for h in range(2):
+            to_chip(d, h).wait_recv()
+            pass_on(d, h).start()
     for d in range(chips):
-        pass_on(d).wait_recv()
+        for h in range(2):
+            pass_on(d, h).wait_recv()
     half = blks // 2
     for j in range(half):
         sg_out[j * rows : (j + 1) * rows] = total[j, :rows]
@@ -311,22 +334,23 @@
 
     for c in w_copies:
         c.wait_send()
-    for d in range(1, chips):
-        to_chip(d).wait_send()
-    for d in range(chips):
-        pass_on(d).wait_send()
-
-    @pl.when(jnp.logical_not(at_middle))
-    def _():
-        to_inner.wait_send()
-
-    @pl.when(at_middle)
-    def _():
-        to_middle.wait_send()
-
-    @pl.when(jnp.logical_not(at_end))
-    def _():
-        to_outer.wait_send()
+    for h in range(2):
+        for d in range(1, chips):
+            to_chip(d, h).wait_send()
+        for d in range(chips):
+            pass_on(d, h).wait_send()
+
+        @pl.when(jnp.logical_not(at_middle))
+        def _():
+            to_inner(h).wait_send()
+
+        @pl.when(at_middle)
+        def _():
+            to_middle(h).wait_send()
+
+        @pl.when(jnp.logical_not(at_end))
+        def _():
+            to_outer(h).wait_send()
 
     for d in range(chips):
         to_sibling(d).wait_send()
@@ -382,8 +406,8 @@
             dma((blks,)),
             dma((2, reps - 1, TR)), dma((2, reps - 1, TR)),
             dma((blks - 1,)), dma((blks - 1,)),
-            dma((3,)), dma((2,)),
-            dma((blks - 1,)), dma((blks - 1,)),
+            dma((3, 2)), dma((2, 2)),
+            dma((blks - 1, 2)), dma((blks - 1, 2)),
             dma((chips,)), dma((chips,)),
             dma((chips - 1,)), dma((chips - 1,)),
         ],

time: 30.4 us -> 30.4 us (level)
  no operation moved by 1% of the time
where the time goes in v3:
time: 30.4 us; the launch traced here: 30.3 us
  Pallas kernels  29.6 us (97%)
  between operations  0.64 us (2%)
    pallas_call x1, Pallas kernels, on_device(): pl.pallas_call(functools.partial(kernel, blks, reps), out_shape=(jax.Shap...  27.8 us
    pallas_call x1, Pallas kernels, on_device(): pl.pallas_call(hand_on, out_shape=tuple((jax.ShapeDtypeStruct(a.shape, a....  1.79 us

profile of v3, /device:TPU:1, one launch (start us, length us, event | category | flops | bytes accessed | tf_op | source)
XLA Modules:
  0.0 30.3 jit_solution(1984970225819474817)
XLA Ops:
  0.6 27.8 %shard_map.120 = (f32[256,128]{1,0:T(8,128)}, f32[128,256]{1,0:T(8,128)}, f32[128,256]{1,0:T(8,128)}, f32[1,256]{1,0:T(1,128)}) custom-call(f32[256,128]{1,0:T(8,128)} %feat.1, f32[256,128]{1,0:T(8,128)} %nm.1, f32[256,256]{1,0:T(8,128)} %og.1, f32[128,256]{1,0:T(8,128)} %ws.1, f32[128,256]{1,0:T(8,128)} %wn.1, f32[1,256]{1,0:T(1,128)} %bitcast.9, ...), custom_call_target="tpu_custom_call" | custom-call | tf_op jit(solution)/shard_map/pallas_call | solution.py:376
  28.5 1.8 %shard_map.121 = (f32[256,128]{1,0:T(8,128)}, f32[128,256]{1,0:T(8,128)}, f32[128,256]{1,0:T(8,128)}, f32[1,256]{1,0:T(1,128)}) custom-call(f32[256,128]{1,0:T(8,128)} %get-tuple-element.12.refs_0_, f32[128,256]{1,0:T(8,128)} %get-tuple-element.13.refs_1_, f32[128,256]{1,0:T(8,128)} %get-tuple-element.14.refs_2_, f32[1,256]{1,0:T(1,128)} %get-tuple-element.15.refs_3_), custom_call_target="tpu_custom_call" | custom-call | tf_op jit(solution)/shard_map/pallas_call | solution.py:423
